TPU v7x, 256 devices: a whole 4x4x8 slice. The times are simulated.
256 devices in a mesh: gx: 8 (over y, x_hi), gy: 32 (over z, x_lo, core).
Axes of the slice: x: 4 (x_hi: 2, x_lo: 2; x = x_hi * 2 + x_lo), y: 4, z: 8, core: 2. Of those that a mesh axis runs over, the one named last changes fastest.
Arguments:
- field: float32 [512, 512, 256], P('gx', 'gy'), may hold values from -6 to 6
- weights: float32 [128, 128, 8, 1024], P('gy', 'gx'), may hold values from -1 to 1
- cotangent: float32 [512, 512, 256], P('gx', 'gy'), may hold values from -6 to 6
Outputs:
- output_field: float32 [512, 512, 256], P('gx', 'gy')
- field_grad: float32 [512, 512, 256], P('gx', 'gy')
- weight_grad: float32 [128, 128, 8, 1024], P('gy', 'gx')
All inputs are finite; a program needn't handle non-finite values.
Results may differ from a plain program's by a relative error of at most 0.000098.
Values sent between devices are 32-bit elements; how exact they have to be, the bound alone decides.
A program may use at most 128 MiB of HBM per device.

v0:
```python
import math

import jax
import jax.numpy as jnp
from jax import lax
from jax.sharding import PartitionSpec as P

NX = 512
NY = 512
MODES = 64
CHANNELS = 32


highest = lax.Precision.HIGHEST


def basis_table(length, row_count, first_cell, modes):
    wave_index = lax.iota(jnp.int32, 2 * modes)[:, None]
    positions = first_cell + lax.iota(jnp.int32, row_count)[None, :]
    frequency = jnp.where(wave_index < modes, wave_index, wave_index - modes + 1)
    phase_steps = frequency * positions % length
    angles = 2.0 * math.pi / length * phase_steps.astype(jnp.float32)
    values = jnp.where(wave_index < modes, jnp.cos(angles), jnp.sin(angles))
    return math.sqrt(2.0 / length) * values


def project_field(source, table_x, table_y):
    row_block = table_x
    xmodes = lax.psum_scatter(
        jnp.einsum("kx,xyc->kyc", row_block, source, precision=highest),
        "gx",
        scatter_dimension=0,
        tiled=True,
    )
    row_block = table_y
    return lax.psum_scatter(
        jnp.einsum("ly,kyc->lkc", row_block, xmodes, precision=highest),
        "gy",
        scatter_dimension=0,
        tiled=True,
    )


def expand_modes(coefs, table_x, table_y):
    row_block = table_y
    partial_y = jnp.einsum(
        "ly,lkc->ykc", row_block, lax.all_gather(coefs, "gy", axis=0, tiled=True), precision=highest
    )
    row_block = table_x
    return jnp.einsum(
        "kx,ykc->xyc",
        row_block,
        lax.all_gather(partial_y, "gx", axis=1, tiled=True),
        precision=highest,
    )


def body(field, weights, cotangent):
    cells_x, cells_y, width = field.shape
    owned_y, owned_x, zcount, square = weights.shape
    table_x = basis_table(NX, cells_x, lax.axis_index("gx") * cells_x, MODES)
    table_y = basis_table(NY, cells_y, lax.axis_index("gy") * cells_y, MODES)
    split_weights = weights.reshape(owned_y, owned_x, zcount, CHANNELS, CHANNELS)
    coefs = project_field(field, table_x, table_y)
    split_coefs = coefs.reshape(owned_y, owned_x, zcount, CHANNELS)
    mixed = jnp.einsum("abzi,abzio->abzo", split_coefs, split_weights, precision=highest)
    output_field = expand_modes(mixed.reshape(owned_y, owned_x, width), table_x, table_y)
    dcoefs = project_field(cotangent, table_x, table_y)
    split_coefs = coefs.reshape(owned_y, owned_x, zcount, CHANNELS)
    split_grads = dcoefs.reshape(owned_y, owned_x, zcount, CHANNELS)
    grad_weights = jnp.einsum("abzi,abzo->abzio", split_coefs, split_grads, precision=highest)
    dmixed = jnp.einsum("abzio,abzo->abzi", split_weights, split_grads, precision=highest)
    weight_grad, dmixed = (
        grad_weights.reshape(owned_y, owned_x, zcount, square),
        dmixed.reshape(owned_y, owned_x, width),
    )
    field_grad = expand_modes(dmixed, table_x, table_y)
    return (output_field, field_grad, weight_grad)


def solution(mesh):
    in_specs = (P("gx", "gy", None), P("gy", "gx", None, None), P("gx", "gy", None))
    out_specs = (P("gx", "gy", None), P("gx", "gy", None), P("gy", "gx", None, None))
    return jax.shard_map(body, mesh=mesh, in_specs=in_specs, out_specs=out_specs, check_vma=False)
```

profile of v0, /device:TPU:1, one launch (start us, length us, event | category | flops | bytes accessed | tf_op | source)
XLA Modules:
  0.0 685.2 jit_solution(9639438831691195312)
XLA Ops:
  7.2 0.0 copy-start
  7.2 0.0 reduce-scatter.9.cloned.1.call-start
  7.3 1.1 copy-done
  8.4 2.5 fusion.4
  10.9 2.6 copy.21
  13.5 0.0 copy-start.2
  13.5 0.0 reduce-scatter.9.cloned.1.call-update
  13.5 0.0 reduce-scatter.5.cloned.1.call-start
  13.6 1.1 copy-done.2
  14.7 2.5 fusion.6
  17.2 2.5 copy.15
  19.8 0.0 reduce-scatter.5.cloned.1.call-update
  19.8 0.0 reduce-scatter.11.cloned.1.call-start
  19.9 76.3 %reduce-scatter.9.cloned.1.call-done = f32[16,16,256]{2,1,0:T(8,128)} async-done(((f32[128,16,256]{2,1,0:T(8,128)}), f32[16,16,256]{2,1,0:T(8,128)}) %reduce-scatter.9.cloned.1.call-update) | async-done | bytes 262160 | tf_op jit(solution)/shard_map/reduce_scatter | solution.py:29
  96.1 2.9 fusion.21
  99.0 2.6 copy.11
  101.6 0.0 reduce-scatter.11.cloned.1.call-update
  101.6 0.2 reduce-scatter.7.cloned.1.call-start
  101.9 77.8 %reduce-scatter.5.cloned.1.call-done = f32[16,16,256]{2,1,0:T(8,128)} async-done(((f32[128,16,256]{2,1,0:T(8,128)}), f32[16,16,256]{2,1,0:T(8,128)}) %reduce-scatter.5.cloned.1.call-update) | async-done | bytes 262160 | tf_op jit(solution)/shard_map/reduce_scatter | solution.py:29
  179.6 2.9 fusion.24
  182.6 2.5 copy.10
  185.1 0.0 copy-start.1
  185.1 0.0 reduce-scatter.7.cloned.1.call-update
  185.1 0.0 all-gather.9.cloned.1.call-start
  185.2 1.5 copy-done.1
  186.7 4.8 reshape.51
  191.5 105.7 %reduce-scatter.11.cloned.1.call-done = f32[4,16,256]{2,1,0:T(8,128)} async-done(((f32[128,16,256]{2,1,0:T(8,128)}), f32[4,16,256]{2,1,0:T(8,128)}) %reduce-scatter.11.cloned.1.call-update) | async-done | bytes 65552 | tf_op jit(solution)/shard_map/reduce_scatter | solution.py:36
  297.2 0.9 reshape.60
  298.1 15.4 %fusion.67 = f32[4,16,8,1,32]{4,3,2,1,0:T(1,128)S(1)} fusion(f32[4,16,8,32,1]{3,4,2,1,0:T(1,128)S(1)} %bitcast.43, f32[4,16,8,32,32]{4,3,2,1,0:T(8,128)} %reshape.51), kind=kOutput, calls=%fused_computation.84 | convolution fusion | flops 6291456 | bytes 2228224 | tf_op jit(solution)/shard_map/abzio,abzo->abzi/dot_general | solution.py:72
  313.5 0.8 reshape.54
  314.3 0.0 all-gather.9.cloned.1.call-update
  314.3 0.3 all-gather.5.cloned.1.call-start
  314.6 102.1 %reduce-scatter.7.cloned.1.call-done = f32[4,16,256]{2,1,0:T(8,128)} async-done(((f32[128,16,256]{2,1,0:T(8,128)}), f32[4,16,256]{2,1,0:T(8,128)}) %reduce-scatter.7.cloned.1.call-update) | async-done | bytes 65552 | tf_op jit(solution)/shard_map/reduce_scatter | solution.py:36
  416.7 0.9 reshape.58
  417.7 9.0 %fusion.66 = f32[4,16,8,1,32]{4,3,2,1,0:T(1,128)S(1)} fusion(f32[4,16,8,32,1]{3,4,2,1,0:T(1,128)S(1)} %bitcast.42, f32[4,16,8,32,32]{4,3,2,1,0:T(8,128)} %reshape.51), kind=kOutput, calls=%fused_computation.83 | convolution fusion | flops 6291456 | bytes 2228224 | tf_op jit(solution)/shard_map/abzi,abzio->abzo/dot_general | solution.py:66
  426.7 0.8 reshape.52
  427.5 0.0 all-gather.5.cloned.1.call-update
  427.5 0.0 all-gather.11.cloned.1.call-start
  427.6 58.2 %all-gather.9.cloned.1.call-done = f32[128,16,256]{2,1,0:T(8,128)} async-done(((f32[4,16,256]{2,1,0:T(8,128)}), f32[128,16,256]{2,1,0:T(8,128)}) %all-gather.9.cloned.1.call-update) | async-done | bytes 2097168 | tf_op jit(solution)/shard_map/all_gather | solution.py:47
  485.7 3.8 fusion
  489.5 0.0 copy-start.3
  489.5 0.0 copy-start.4
  489.6 0.9 copy.25
  490.4 0.0 all-gather.11.cloned.1.call-update
  490.4 0.3 all-gather.7.cloned.1.call-start
  490.8 61.7 %all-gather.5.cloned.1.call-done = f32[128,16,256]{2,1,0:T(8,128)} async-done(((f32[4,16,256]{2,1,0:T(8,128)}), f32[128,16,256]{2,1,0:T(8,128)}) %all-gather.5.cloned.1.call-update) | async-done | bytes 2097168 | tf_op jit(solution)/shard_map/all_gather | solution.py:47
  552.5 3.8 fusion.2
  556.3 0.9 copy.19
  557.1 0.0 all-gather.7.cloned.1.call-update
  557.1 0.0 copy-done.3
  557.1 0.1 reshape.53
  557.3 0.0 copy-done.4
  557.3 0.1 reshape.50
  557.4 4.6 broadcast_multiply_fusion
  561.9 7.8 %reshape.55 = f32[4,16,8,1024]{3,2,1,0:T(8,128)} reshape(f32[4,16,8,32,32]{4,3,2,1,0:T(8,128)} %broadcast_multiply_fusion) | data formatting | bytes 4194304 | tf_op jit(solution)/shard_map/reshape | solution.py:74
  569.7 43.9 %all-gather.11.cloned.1.call-done = f32[16,128,256]{2,1,0:T(8,128)} async-done(((f32[16,16,256]{2,1,0:T(8,128)}), f32[16,128,256]{2,1,0:T(8,128)}) %all-gather.11.cloned.1.call-update) | async-done | bytes 2097168 | tf_op jit(solution)/shard_map/all_gather | solution.py:53
  613.6 3.0 fusion.11
  616.6 1.6 copy.13
  618.2 55.6 %all-gather.7.cloned.1.call-done = f32[16,128,256]{2,1,0:T(8,128)} async-done(((f32[16,16,256]{2,1,0:T(8,128)}), f32[16,128,256]{2,1,0:T(8,128)}) %all-gather.7.cloned.1.call-update) | async-done | bytes 2097168 | tf_op jit(solution)/shard_map/all_gather | solution.py:53
  673.8 3.0 fusion.14
  676.8 1.6 copy.12
  (4 shorter events, 0.0 us)
Async XLA Ops:
  7.2 1.2 copy-start
  7.2 88.9 %reduce-scatter.9.cloned.1.call-start = ((), (), s32[]{:S(2)}) async-start(), calls=%async_computation.8 | async-start | bytes 2359296 | tf_op jit(solution)/shard_map/reduce_scatter | solution.py:29
  13.5 1.2 copy-start.2
  13.5 166.1 %reduce-scatter.5.cloned.1.call-start = ((), (), s32[]{:S(2)}) async-start(), calls=%async_computation.4 | async-start | bytes 2359296 | tf_op jit(solution)/shard_map/reduce_scatter | solution.py:29
  19.8 277.4 %reduce-scatter.11.cloned.1.call-start = ((), (), s32[]{:S(2)}) async-start(), calls=%async_computation.9 | async-start | bytes 2162688 | tf_op jit(solution)/shard_map/reduce_scatter | solution.py:36
  101.6 315.1 %reduce-scatter.7.cloned.1.call-start = ((), (), s32[]{:S(2)}) async-start(), calls=%async_computation.5 | async-start | bytes 2162688 | tf_op jit(solution)/shard_map/reduce_scatter | solution.py:36
  185.1 1.6 copy-start.1
  185.1 300.6 %all-gather.9.cloned.1.call-start = ((), (), s32[]{:S(2)}) async-start(), calls=%async_computation.10 | async-start | bytes 2162688 | tf_op jit(solution)/shard_map/all_gather | solution.py:47
  314.3 238.1 %all-gather.5.cloned.1.call-start = ((), (), s32[]{:S(2)}) async-start(), calls=%async_computation.6 | async-start | bytes 2162688 | tf_op jit(solution)/shard_map/all_gather | solution.py:47
  427.5 186.1 %all-gather.11.cloned.1.call-start = ((), (), s32[]{:S(2)}) async-start(), calls=%async_computation.11 | async-start | bytes 2359296 | tf_op jit(solution)/shard_map/all_gather | solution.py:53
  489.5 67.6 %copy-start.3 = (f32[4,16,256]{2,1,0:T(8,128)S(1)}, f32[4,16,256]{2,1,0:T(8,128)}, u32[]{:S(2)}) copy-start(f32[4,16,256]{2,1,0:T(8,128)} %reduce-scatter.11.cloned.1.call-done) | copy-start | bytes 196612
  489.5 67.7 %copy-start.4 = (f32[4,16,256]{2,1,0:T(8,128)S(1)}, f32[4,16,256]{2,1,0:T(8,128)}, u32[]{:S(2)}) copy-start(f32[4,16,256]{2,1,0:T(8,128)} %reduce-scatter.7.cloned.1.call-done) | copy-start | bytes 196612
  490.4 183.3 %all-gather.7.cloned.1.call-start = ((), (), s32[]{:S(2)}) async-start(), calls=%async_computation.7 | async-start | bytes 2359296 | tf_op jit(solution)/shard_map/all_gather | solution.py:53
Sparse Core Ops, SparseCore 0:
  13.6 82.4 reduce-scatter.8
  100.7 78.9 reduce-scatter.4
  182.2 114.9 reduce-scatter.10
  300.3 116.4 reduce-scatter.6
  419.0 66.6 all-gather.8
  488.0 64.3 all-gather.4
  555.6 57.9 all-gather.10
  616.8 56.9 all-gather.6
where the time goes:
time: 686 us; the launch traced here: 685 us
  waiting for transfers between devices  581 us (85%)
  matrix products  48.9 us (7%)
  local copies, waits for them, and re-layouts  35.1 us (5%)
  between operations  14.3 us (2%)
    reduce_scatter x2, waiting for transfers between devices, project_field(): lax.psum_scatter(jnp.einsum('ly,kyc->lkc', row_block, xmodes, precision=h...  208 us
    reduce_scatter x2, waiting for transfers between devices, project_field(): lax.psum_scatter(jnp.einsum('kx,xyc->kyc', row_block, source, precision=h...  154 us
    all_gather x2, waiting for transfers between devices, expand_modes(): lax.all_gather(coefs, 'gy', axis=0, tiled=True)  120 us
    all_gather x2, waiting for transfers between devices, expand_modes(): lax.all_gather(partial_y, 'gx', axis=1, tiled=True)  99.5 us
    dot_general x1, matrix products, body(): jnp.einsum('abzio,abzo->abzi', split_weights, split_grads, precision=high...  15.4 us
  transfers between devices with their start and end apart: 8, of which 8 were waited for; matrix products, arithmetic and copies ran while one was open for 11% of the time, Pallas kernels for 0%

commit v1 on v0

v1 whole, which is shorter than its diff:
```python
import math

import jax
import jax.numpy as jnp
from jax import lax
from jax.sharding import PartitionSpec as P

NX = 512
NY = 512
MODES = 64
CHANNELS = 32


high = lax.Precision.HIGH


def basis_table(length, modes):
    wave_index = lax.iota(jnp.int32, 2 * modes)[:, None]
    positions = lax.iota(jnp.int32, length)[None, :]
    frequency = jnp.where(wave_index < modes, wave_index, wave_index - modes + 1)
    phase_steps = frequency * positions % length
    angles = 2.0 * math.pi / length * phase_steps.astype(jnp.float32)
    values = jnp.where(wave_index < modes, jnp.cos(angles), jnp.sin(angles))
    return math.sqrt(2.0 / length) * values


def project(pair, table_x, table_y):
    cells = lax.all_to_all(pair, "gx", split_axis=3, concat_axis=1, tiled=True)
    xmodes = jnp.einsum("kx,fxyc->fkyc", table_x, cells, precision=high)
    columns = lax.all_to_all(xmodes, "gy", split_axis=1, concat_axis=2, tiled=True)
    modes = jnp.einsum("ly,fkyc->flkc", table_y, columns, precision=high)
    owned = lax.all_to_all(modes, "gy", split_axis=1, concat_axis=2, tiled=True)
    return lax.all_to_all(owned, "gx", split_axis=2, concat_axis=3, tiled=True)


def expand(pair, table_x, table_y):
    owned = lax.all_to_all(pair, "gx", split_axis=3, concat_axis=2, tiled=True)
    modes = lax.all_to_all(owned, "gy", split_axis=2, concat_axis=1, tiled=True)
    columns = jnp.einsum("ly,flkc->fkyc", table_y, modes, precision=high)
    xmodes = lax.all_to_all(columns, "gy", split_axis=2, concat_axis=1, tiled=True)
    cells = jnp.einsum("kx,fkyc->fxyc", table_x, xmodes, precision=high)
    return lax.all_to_all(cells, "gx", split_axis=1, concat_axis=3, tiled=True)


def body(field, weights, cotangent):
    owned_y, owned_x, zcount, square = weights.shape
    width = field.shape[2]
    table_x = basis_table(NX, MODES)
    table_y = basis_table(NY, MODES)
    split_weights = weights.reshape(owned_y, owned_x, zcount, CHANNELS, CHANNELS)
    both = project(jnp.stack([field, cotangent]), table_x, table_y)
    both = both.reshape(2, owned_y, owned_x, zcount, CHANNELS)
    coefs, grads = both[0], both[1]
    mixed = jnp.einsum("abzi,abzio->abzo", coefs, split_weights, precision=lax.Precision.HIGHEST)
    dmixed = jnp.einsum("abzio,abzo->abzi", split_weights, grads, precision=lax.Precision.HIGHEST)
    weight_grad = coefs[..., :, None] * grads[..., None, :]
    back = jnp.stack([mixed, dmixed]).reshape(2, owned_y, owned_x, width)
    out = expand(back, table_x, table_y)
    return out[0], out[1], weight_grad.reshape(weights.shape)


def solution(mesh):
    in_specs = (P("gx", "gy", None), P("gy", "gx", None, None), P("gx", "gy", None))
    out_specs = (P("gx", "gy", None), P("gx", "gy", None), P("gy", "gx", None, None))
    return jax.shard_map(body, mesh=mesh, in_specs=in_specs, out_specs=out_specs, check_vma=False)
```

time: 686 us -> 313 us (0.46)
  waiting for transfers between devices: 581 us -> 44.3 us
  blocking collectives: 0 us -> 87 us
  local copies, waits for them, and re-layouts: 35.1 us -> 94.4 us
  other arithmetic: 4.57 us -> 30.5 us
  starting transfers between devices: 0.99 us -> 16.1 us
  matrix products: 48.9 us -> 34.4 us
  between operations: 14.3 us -> 1.27 us
    reduce_scatter x4 -> x0, waiting for transfers between devices: 362 us -> none  [the longest x2 208 us: project_field(): lax.psum_scatter(jnp.einsum('ly,kyc->lkc', row_block, xmodes, precision=h...]
    all_gather x4 -> x0, waiting for transfers between devices: 219 us -> none  [the longest x2 120 us: expand_modes(): lax.all_gather(coefs, 'gy', axis=0, tiled=True)]
    all_to_all x0 -> x5, blocking collectives: none -> 87 us  [the longest x1 27.1 us: project(): lax.all_to_all(xmodes, 'gy', split_axis=1, concat_axis=2, tiled=True)]
    all_to_all x0 -> x3, waiting for transfers between devices: none -> 44.3 us  [the longest x1 27.5 us: project(): cells = lax.all_to_all(pair, 'gx', split_axis=3, concat_axis=1, tiled=True)]
    unnamed x12 -> x26, local copies, waits for them, and re-layouts: 6.97 us -> 45.4 us
    all_to_all x0 -> x8, other arithmetic: none -> 22 us  [the longest x1 7.22 us: expand(): return lax.all_to_all(cells, 'gx', split_axis=1, concat_axis=3, tiled=True)]
    all_to_all x0 -> x15, local copies, waits for them, and re-layouts: none -> 20.6 us  [the longest x3 10.7 us: project(): cells = lax.all_to_all(pair, 'gx', split_axis=3, concat_axis=1, tiled=True)]
    all_to_all x0 -> x3, starting transfers between devices: none -> 16.1 us  [the longest x1 7.97 us: project(): cells = lax.all_to_all(pair, 'gx', split_axis=3, concat_axis=1, tiled=True)]
  transfers between devices with their start and end apart: 8 -> 3, of which waited for: 8 -> 3; matrix products, arithmetic and copies ran while one was open for 11% -> 6% of each run, Pallas kernels for 0% -> 0%
where the time goes in v1:
time: 313 us; the launch traced here: 308 us
  local copies, waits for them, and re-layouts  94.4 us (30%)
  blocking collectives  87 us (28%)
  waiting for transfers between devices  44.3 us (14%)
  matrix products  34.4 us (11%)
  other arithmetic  30.5 us (10%)
  starting transfers between devices  16.1 us (5%)
    unnamed x26, local copies, waits for them, and re-layouts  45.4 us
    all_to_all x1, waiting for transfers between devices, project(): cells = lax.all_to_all(pair, 'gx', split_axis=3, concat_axis=1, tiled=True)  27.5 us
    all_to_all x1, blocking collectives, project(): lax.all_to_all(xmodes, 'gy', split_axis=1, concat_axis=2, tiled=True)  27.1 us
    all_to_all x1, blocking collectives, expand(): lax.all_to_all(columns, 'gy', split_axis=2, concat_axis=1, tiled=True)  20.4 us
    dot_general x1, matrix products, body(): jnp.einsum('abzio,abzo->abzi', split_weights, grads, precision=lax.Precis...  15.4 us
    all_to_all x1, waiting for transfers between devices, expand(): return lax.all_to_all(cells, 'gx', split_axis=1, concat_axis=3, tiled=True)  14.7 us
    all_to_all x1, blocking collectives, expand(): modes = lax.all_to_all(owned, 'gy', split_axis=2, concat_axis=1, tiled=True)  14.3 us
    all_to_all x1, blocking collectives, project(): owned = lax.all_to_all(modes, 'gy', split_axis=1, concat_axis=2, tiled=True)  13.5 us
  transfers between devices with their start and end apart: 3, of which 3 were waited for; matrix products, arithmetic and copies ran while one was open for 6% of the time, Pallas kernels for 0%

profile of v1, /device:TPU:1, one launch (start us, length us, event | category | flops | bytes accessed | tf_op | source)
XLA Modules:
  0.0 308.1 jit_solution(3926754128686557113)
XLA Ops:
  0.6 2.8 copy.77
  3.5 2.7 copy.78
  6.2 3.9 %fusion.40 = f32[256,2,16,64]{3,2,1,0:T(8,128)} fusion(f32[1,64,16,256]{1,2,0,3:T(8,128)} %bitcast.116, f32[1,64,16,256]{1,2,0,3:T(8,128)S(1)} %bitcast.115), kind=kLoop, calls=%fused_computation.54 | loop fusion | flops 524288 | bytes 4194304
  10.1 7.2 %reshape.49 = f32[8,1,65536]{2,1,0:T(1,128)} reshape(f32[256,2,16,64]{3,2,1,0:T(8,128)} %fusion.40) | data formatting | bytes 4194304
  17.3 8.0 %all-to-all-start = ((f32[8,1,65536]{2,1,0:T(1,128)}), f32[8,1,65536]{2,1,0:T(1,128)S(1)}, u32[]{:S(2)}, u32[]{:S(2)}) async-start(f32[8,1,65536]{2,1,0:T(1,128)} %reshape.49), calls=%async_computation | async-start | bytes 4194304 | tf_op jit(solution)/shard_map/all_to_all | solution.py:28
  25.3 27.5 %all-to-all-done = f32[8,1,65536]{2,1,0:T(1,128)S(1)} async-done(((f32[8,1,65536]{2,1,0:T(1,128)}), f32[8,1,65536]{2,1,0:T(1,128)S(1)}, u32[]{:S(2)}, u32[]{:S(2)}) %all-to-all-start) | async-done | bytes 2097184 | tf_op jit(solution)/shard_map/all_to_all | solution.py:28
  52.8 1.3 copy-done
  54.1 0.5 broadcast.82
  54.6 7.2 %reduce = f32[8,65536]{1,0:T(8,128)S(1)} reduce(f32[8,1,65536]{2,1,0:T(1,128)} %copy-done, f32[]{:T(128)} %broadcast.82), dimensions={1}, to_apply=%all_to_all.100.reduce_sub_computation | reduce | bytes 4194308 | tf_op jit(solution)/shard_map/all_to_all | solution.py:28
  61.8 3.6 %reshape.50 = f32[256,2,16,64]{3,2,1,0:T(8,128)} reshape(f32[8,65536]{1,0:T(8,128)S(1)} %reduce) | data formatting | bytes 4194304
  65.4 6.6 %copy.80 = f32[2,8,64,16,32]{2,1,4,3,0:T(8,128)} copy(f32[2,8,64,16,32]{2,3,0,4,1:T(8,128)} %bitcast.105) | data formatting | bytes 4194304 | tf_op jit(solution)/shard_map/all_to_all | solution.py:28
  72.0 3.6 %all_to_all.103 = f32[2,512,16,32]{1,3,2,0:T(8,128)S(1)} reshape(f32[2,8,64,16,32]{2,1,4,3,0:T(8,128)} %copy.80) | data formatting | bytes 4194304 | tf_op jit(solution)/shard_map/all_to_all | solution.py:28
  75.6 2.1 convolution_bitcast_fusion.1
  77.7 1.8 copy.81
  79.5 0.9 reshape.51
  80.5 27.1 %all_to_all.138 = f32[32,1,4096]{2,1,0:T(1,128)S(1)} all-to-all(f32[32,1,4096]{2,1,0:T(1,128)S(1)} %reshape.51), channel_id=1, replica_groups=mesh['gx'=8,'gy'=32] {'gy'}, dimensions={0} | all-to-all | bytes 1048576 | tf_op jit(solution)/shard_map/all_to_all | solution.py:30
  107.5 1.9 reduce.1
  109.4 0.7 reshape.52
  110.3 2.8 convolution_bitcast_fusion.2
  113.1 0.3 copy.85
  113.4 0.3 reshape.53
  113.7 13.5 %all_to_all.139 = f32[32,1,1024]{2,1,0:T(1,128)S(1)} all-to-all(f32[32,1,1024]{2,1,0:T(1,128)S(1)} %reshape.53), channel_id=1, replica_groups=mesh['gx'=8,'gy'=32] {'gy'}, dimensions={0} | all-to-all | bytes 262144 | tf_op jit(solution)/shard_map/all_to_all | solution.py:32
  127.3 1.0 reduce.2
  128.6 0.3 copy.87
  129.0 0.3 copy.129
  129.3 1.0 reshape.55
  130.3 3.6 %all-to-all-start.3 = ((f32[8,1,4096]{2,1,0:T(1,128)}), f32[8,1,4096]{2,1,0:T(1,128)S(1)}, u32[]{:S(2)}, u32[]{:S(2)}) async-start(f32[8,1,4096]{2,1,0:T(1,128)} %reshape.55), calls=%async_computation.3 | async-start | bytes 262144 | tf_op jit(solution)/shard_map/all_to_all | solution.py:33
  133.9 4.8 %reshape.43 = f32[4,16,8,32,32]{4,3,2,1,0:T(8,128)} reshape(f32[4,16,8,1024]{3,2,1,0:T(8,128)S(1)} %copy-done.1) | data formatting | bytes 4194304 | tf_op jit(solution)/shard_map/reshape | solution.py:50
  138.7 2.2 all-to-all-done.3
  140.9 1.0 reduce.3
  142.3 9.1 %fusion.14 = f32[4,16,8,1,32]{4,3,2,1,0:T(1,128)S(1)} fusion(f32[4,16,8,32,32]{4,3,2,1,0:T(8,128)} %reshape.43, f32[4,16,8,32,1]{3,1,2,0,4:T(8,128)S(1)} %get-tuple-element.18), kind=kOutput, calls=%fused_computation.20 | convolution fusion | flops 6291456 | bytes 2228224 | tf_op jit(solution)/shard_map/abzi,abzio->abzo/dot_general | solution.py:54
  151.6 15.4 %fusion.12 = f32[4,16,8,1,32]{4,3,2,1,0:T(1,128)S(1)} fusion(f32[4,16,8,32,32]{4,3,2,1,0:T(8,128)} %reshape.43, f32[4,16,8,32,1]{3,1,2,0,4:T(8,128)S(1)} %get-tuple-element.19), kind=kOutput, calls=%fused_computation.18 | convolution fusion | flops 6291456 | bytes 2228224 | tf_op jit(solution)/shard_map/abzio,abzo->abzi/dot_general | solution.py:55
  167.1 0.5 copy.90
  167.6 0.8 reshape.57
  168.4 11.7 %all_to_all.140 = f32[8,1,4096]{2,1,0:T(1,128)S(1)} all-to-all(f32[8,1,4096]{2,1,0:T(1,128)S(1)} %reshape.57), channel_id=1, replica_groups=mesh['gx'=8,'gy'=32] {'gx'}, dimensions={0} | all-to-all | bytes 262144 | tf_op jit(solution)/shard_map/all_to_all | solution.py:37
  180.1 1.0 reduce.4
  181.1 0.7 reshape.58
  181.8 0.5 copy.117
  182.3 0.3 copy.128
  182.7 0.3 reshape.59
  183.0 14.3 %all_to_all.141 = f32[32,1,1024]{2,1,0:T(1,128)S(1)} all-to-all(f32[32,1,1024]{2,1,0:T(1,128)S(1)} %reshape.59), channel_id=1, replica_groups=mesh['gx'=8,'gy'=32] {'gy'}, dimensions={0} | all-to-all | bytes 262144 | tf_op jit(solution)/shard_map/all_to_all | solution.py:38
  197.3 1.0 reduce.5
  198.6 0.3 copy.95
  199.0 1.6 convolution_bitcast_fusion
  200.6 1.1 copy.97
  201.7 1.4 reshape.61
  203.1 20.4 %all_to_all.142 = f32[32,1,4096]{2,1,0:T(1,128)S(1)} all-to-all(f32[32,1,4096]{2,1,0:T(1,128)S(1)} %reshape.61), channel_id=1, replica_groups=mesh['gx'=8,'gy'=32] {'gy'}, dimensions={0} | all-to-all | bytes 1048576 | tf_op jit(solution)/shard_map/all_to_all | solution.py:40
  223.5 1.9 reduce.6
  225.4 1.1 reshape.62
  226.5 0.4 copy.98
  226.9 0.3 copy.99
  227.2 3.4 %fusion.2 = f32[2,512,16,32]{1,3,2,0:T(8,128)S(1)} fusion(f32[2,128,16,32]{3,2,1,0:T(8,128)S(1)} %bitcast.108, s32[128]{0:T(128)S(1)} %add_select_fusion.1, pred[128]{0:T(512)(128)(4,1)S(1)} %iota_compare_fusion), kind=kOutput, calls=%fused_computation.4 | convolution fusion | flops 403701760 | bytes 2622080 | tf_op jit(solution)/shard_map/kx,fkyc->fxyc/dot_general | solution.py:41
  230.6 7.6 %copy.101 = f32[2,512,16,32]{3,2,0,1:T(8,128)} copy(f32[2,512,16,32]{1,3,2,0:T(8,128)S(1)} %fusion.2) | data formatting | bytes 4194304 | tf_op jit(solution)/shard_map/kx,fkyc->fxyc/transpose | solution.py:41
  238.2 8.6 %reshape.63 = f32[8,1,65536]{2,1,0:T(1,128)} reshape(f32[512,2,16,32]{3,2,1,0:T(8,128)} %bitcast.102) | data formatting | bytes 4194304
  246.8 4.6 %all-to-all-start.7 = ((f32[8,1,65536]{2,1,0:T(1,128)}), f32[8,1,65536]{2,1,0:T(1,128)}, u32[]{:S(2)}, u32[]{:S(2)}) async-start(f32[8,1,65536]{2,1,0:T(1,128)} %reshape.63), calls=%async_computation.7 | async-start | bytes 4194304 | tf_op jit(solution)/shard_map/all_to_all | solution.py:42
  251.5 4.6 %broadcast_multiply_fusion = f32[4,16,8,32,32]{4,3,2,1,0:T(8,128)} fusion(f32[4,16,8,32]{3,2,1,0:T(8,128)S(1)} %copy.104, f32[4,16,8,32]{3,2,1,0:T(8,128)S(1)} %copy.103), kind=kLoop, calls=%fused_computation.1 | loop fusion | flops 524288 | bytes 2228224 | tf_op jit(solution)/shard_map/mul | solution.py:56
  256.1 7.7 %mul.83 = f32[4,16,8,1024]{3,2,1,0:T(8,128)} reshape(f32[4,16,8,32,32]{4,3,2,1,0:T(8,128)} %broadcast_multiply_fusion) | data formatting | bytes 4194304 | tf_op jit(solution)/shard_map/mul | solution.py:56
  263.8 14.7 %all-to-all-done.7 = f32[8,1,65536]{2,1,0:T(1,128)} async-done(((f32[8,1,65536]{2,1,0:T(1,128)}), f32[8,1,65536]{2,1,0:T(1,128)}, u32[]{:S(2)}, u32[]{:S(2)}) %all-to-all-start.7) | async-done | bytes 2097184 | tf_op jit(solution)/shard_map/all_to_all | solution.py:42
  278.5 7.2 %reduce.7 = f32[8,65536]{1,0:T(8,128)S(1)} reduce(f32[8,1,65536]{2,1,0:T(1,128)} %all-to-all-done.7, f32[]{:T(128)} %broadcast.82), dimensions={1}, to_apply=%all_to_all.127.reduce_sub_computation | reduce | bytes 4194308 | tf_op jit(solution)/shard_map/all_to_all | solution.py:42
  285.7 6.0 %reshape.64 = f32[512,2,16,32]{3,2,1,0:T(8,128)} reshape(f32[8,65536]{1,0:T(8,128)S(1)} %reduce.7) | data formatting | bytes 4194304
  291.7 6.8 %copy.102 = f32[2,8,64,16,32]{2,4,1,3,0:T(8,128)} copy(f32[2,8,64,16,32]{4,3,0,2,1:T(8,128)} %bitcast.103) | data formatting | bytes 4194304 | tf_op jit(solution)/shard_map/all_to_all | solution.py:42
  298.5 4.2 %fusion.39 = (f32[1,64,16,8,32]{1,4,3,2,0:T(8,128)S(1)}, f32[1,64,16,8,32]{1,4,3,2,0:T(8,128)}) fusion(f32[2,64,16,8,32]{1,4,3,2,0:T(8,128)} %bitcast.104), kind=kLoop, calls=%fused_computation.53 | loop fusion | bytes 4194304 | tf_op jit(solution)/shard_map/slice | solution.py:59
  302.7 3.4 %copy.105 = f32[64,16,256]{2,1,0:T(8,128)} copy(f32[64,16,256]{0,2,1:T(8,128)} %bitcast.114) | data formatting | bytes 2097152
  306.1 1.8 copy.106
  (20 shorter events, 1.8 us)
Async XLA Ops:
  0.6 2.8 copy-start.2
  17.3 35.5 %all-to-all-start = ((f32[8,1,65536]{2,1,0:T(1,128)}), f32[8,1,65536]{2,1,0:T(1,128)S(1)}, u32[]{:S(2)}, u32[]{:S(2)}) async-start(f32[8,1,65536]{2,1,0:T(1,128)} %reshape.49), calls=%async_computation | async-start | bytes 4194304 | tf_op jit(solution)/shard_map/all_to_all | solution.py:28
  52.8 1.3 copy-start
  128.5 5.4 %copy-start.1 = (f32[4,16,8,1024]{3,2,1,0:T(8,128)S(1)}, f32[4,16,8,1024]{3,2,1,0:T(8,128)}, u32[]{:S(2)}) copy-start(f32[4,16,8,1024]{3,2,1,0:T(8,128)} %param.4) | copy-start | bytes 6291460
  130.3 10.6 %all-to-all-start.3 = ((f32[8,1,4096]{2,1,0:T(1,128)}), f32[8,1,4096]{2,1,0:T(1,128)S(1)}, u32[]{:S(2)}, u32[]{:S(2)}) async-start(f32[8,1,4096]{2,1,0:T(1,128)} %reshape.55), calls=%async_computation.3 | async-start | bytes 262144 | tf_op jit(solution)/shard_map/all_to_all | solution.py:33
  246.8 31.7 %all-to-all-start.7 = ((f32[8,1,65536]{2,1,0:T(1,128)}), f32[8,1,65536]{2,1,0:T(1,128)}, u32[]{:S(2)}, u32[]{:S(2)}) async-start(f32[8,1,65536]{2,1,0:T(1,128)} %reshape.63), calls=%async_computation.7 | async-start | bytes 4194304 | tf_op jit(solution)/shard_map/all_to_all | solution.py:42

commit v2 on v1

v2 whole, which is shorter than its diff:
```python
import math

import jax
import jax.numpy as jnp
import numpy as np
from jax import lax
from jax.experimental import pallas as pl
from jax.experimental.pallas import tpu as pltpu
from jax.sharding import PartitionSpec as P

N = 512
MODES = 64
GX = 8
GY = 32
F32 = jnp.float32
BF16 = jnp.bfloat16
MESH = pl.DeviceIdType.MESH


def basis_table():
    k = np.arange(2 * MODES)[:, None]
    p = np.arange(N)[None, :]
    frequency = np.where(k < MODES, k, k - MODES + 1)
    angles = 2.0 * math.pi / N * ((frequency * p) % N)
    values = math.sqrt(2.0 / N) * np.where(k < MODES, np.cos(angles), np.sin(angles))
    return values.reshape(32, 4, N).transpose(1, 0, 2).reshape(128, N)


def split_table(values):
    values = values.astype(np.float32)
    high = values.astype(BF16)
    low = (values - high.astype(np.float32)).astype(BF16)
    return high, low


def halves(value):
    high = value.astype(BF16)
    return high, (value - high.astype(F32)).astype(BF16)


def dot(a, b):
    return jnp.dot(a, b, preferred_element_type=F32)


def swap_blocks(v):
    lane = lax.broadcasted_iota(jnp.int32, v[0].shape, 1)
    low = lane < 64
    even = (lane // 32) % 2 == 0
    a0 = jnp.where(low, v[0], pltpu.roll(v[2], 64, 1))
    a1 = jnp.where(low, v[1], pltpu.roll(v[3], 64, 1))
    a2 = jnp.where(low, pltpu.roll(v[0], 64, 1), v[2])
    a3 = jnp.where(low, pltpu.roll(v[1], 64, 1), v[3])
    return [
        jnp.where(even, a0, pltpu.roll(a1, 32, 1)),
        jnp.where(even, pltpu.roll(a0, 96, 1), a1),
        jnp.where(even, a2, pltpu.roll(a3, 32, 1)),
        jnp.where(even, pltpu.roll(a2, 96, 1), a3),
    ]


def kernel(
    field, cotangent, weights, table_in, table_out,
    output_field, field_grad, weight_grad,
    cells, w, fwd, inv, spread, expanded, wgrad, result,
    sa, ra, sb, rb, sc, rc, sd, rd, se, re, sf, rf,
    in_sem, out_sem, a_send, a_recv, b_send, b_recv, c_send, c_recv,
    d_send, d_recv, e_send, e_recv, f_send, f_recv,
):
    i = lax.axis_index("gx")
    j = lax.axis_index("gy")

    def at(gx, gy):
        return {"gx": gx, "gy": gy}

    loads = [
        pltpu.make_async_copy(src, dst, in_sem.at[n])
        for n, (src, dst) in enumerate(
            [(field, cells.at[0]), (cotangent, cells.at[1]), (table_in, fwd), (weights, w), (table_out, inv)]
        )
    ]
    for load in loads:
        load.start()

    barrier = pltpu.get_barrier_semaphore()

    def greet(gx, gy):
        pl.semaphore_signal(barrier, inc=1, device_id=at(gx, gy), device_id_type=MESH)

    def greet_x(v, carry):
        greet((i + v) % GX, j)
        return carry

    def greet_y(v, carry):
        other = (j + v) % GY
        greet(i, other)
        greet(j // 4, other)
        greet((i + v // 4) % GX, 4 * i + v % 4)
        return carry

    lax.fori_loop(0, GX, greet_x, 0)
    lax.fori_loop(0, GY, greet_y, 0)

    def send(src, dst, send_sem, recv_sem, gx, gy):
        here = jnp.logical_and(gx == i, gy == j)

        @pl.when(jnp.logical_not(here))
        def _():
            pltpu.make_async_remote_copy(
                src_ref=src, dst_ref=dst, send_sem=send_sem, recv_sem=recv_sem,
                device_id=at(gx, gy), device_id_type=MESH,
            ).start()

        @pl.when(here)
        def _():
            pltpu.make_async_copy(src, dst, recv_sem).start()

    def wait(ref, sem):
        pltpu.make_async_copy(ref, ref, sem).wait()

    def pack_cells(n, u):
        for t in range(2):
            for h in range(2):
                v = [cells[n, :, 8 * u + 4 * t + s, pl.ds(128 * h, 128)] for s in range(4)]
                for b, value in enumerate(swap_blocks(v)):
                    sa[n, u, 4 * h + b, :, pl.ds(128 * t, 128)] = value

    def send_cells(n, u):
        def step(v, carry):
            other = (i + v) % GX
            send(sa.at[n, u, other], ra.at[n, u, i], a_send.at[n, u], a_recv.at[n, u], other, j)
            return carry

        lax.fori_loop(0, GX, step, 0)

    def project(data):
        high, low = halves(data)
        first = dot(fwd[...], high)
        return first[:128] + first[128:] + dot(fwd[:128], low)

    def expand(data):
        high, low = halves(data)
        return dot(inv[...], jnp.concatenate([high, high, low], axis=0))

    def project_x(n, u):
        wait(ra.at[n, u], a_recv.at[n, u])
        modes = project(ra[n, u].reshape(N, 256))
        for t in range(2):
            v = [modes[32 * r : 32 * r + 32, 128 * t : 128 * t + 128] for r in range(4)]
            for s, value in enumerate(swap_blocks(v)):
                sb[n, :, 8 * u + 4 * t + s, :] = value

    def send_columns(n, src, dst, send_sem, recv_sem):
        def step(v, carry):
            other = (j + v) % GY
            send(src.at[n, other], dst.at[n, j], send_sem.at[n], recv_sem.at[n], i, other)
            return carry

        lax.fori_loop(0, GY, step, 0)

    def project_y(n):
        wait(rb.at[n], b_recv.at[n])
        modes = project(rb[n].reshape(N, 128))
        for a in range(4):
            sc[n, :, a, :] = modes[32 * a : 32 * a + 32]

        def step(v, carry):
            other = (j + v) % GY
            send(sc.at[n, other], rc.at[n, i, j % 4], c_send.at[n], c_recv.at[n], j // 4, other)
            return carry

        lax.fori_loop(0, GY, step, 0)

    def owned_modes(n):
        wait(rc.at[n], c_recv.at[n])
        return jnp.concatenate([rc[n, :, q, a, :] for a in range(4) for q in range(4)], axis=0)

    def send_mixed(n, value):
        for a in range(4):
            for q in range(4):
                row = 8 * (4 * a + q)
                sd[n, :, q, a, :] = value[row : row + 8]

        def step(v, carry):
            z = (i + v // 4) % GX
            q = v % 4
            send(sd.at[n, z, q], rd.at[n, j], d_send.at[n], d_recv.at[n], z, 4 * i + q)
            return carry

        lax.fori_loop(0, GY, step, 0)

    def mix():
        high, low = halves(owned_modes(0))
        folded = []
        for r in range(4):
            part = spread[:, pl.ds(1024 * r, 1024)]
            wide = dot(high, part) + dot(low, part)
            expanded[:, pl.ds(1024 * r, 1024)] = wide
            product = wide * w[:, :, r].reshape(128, 1024)
            total = product[:, :128]
            for t in range(1, 8):
                total = total + product[:, 128 * t : 128 * t + 128]
            folded.append(total)
        parts = swap_blocks(folded)
        send_mixed(0, (parts[0] + parts[1]) + (parts[2] + parts[3]))

    def mix_back():
        grads = owned_modes(1)
        tiled = swap_blocks([grads] * 4)
        total = None
        for r in range(4):
            part = spread[:, pl.ds(1024 * r, 1024)]
            product = w[:, :, r].reshape(128, 1024) * jnp.concatenate([tiled[r]] * 8, axis=1)
            high, low = halves(product)
            dims = (((1,), (1,)), ((), ()))
            term = lax.dot_general(high, part, dims, preferred_element_type=F32)
            term = term + lax.dot_general(low, part, dims, preferred_element_type=F32)
            total = term if total is None else total + term
        send_mixed(1, total)
        return tiled

    def outer(tiled):
        for r in range(4):
            value = expanded[:, pl.ds(1024 * r, 1024)] * jnp.concatenate([tiled[r]] * 8, axis=1)
            wgrad[:, :, r] = value.reshape(4, 4, 8, 1024)

    def expand_y(n):
        wait(rd.at[n], d_recv.at[n])
        modes = jnp.concatenate([rd[n, :, a, :] for a in range(4)], axis=0)
        se[n] = expand(modes).reshape(GY, 16, 128)
        send_columns(n, se, re, e_send, e_recv)

    def expand_x(n, u):
        rows = [[] for _ in range(4)]
        for t in range(2):
            v = [re[n, :, 8 * u + 4 * t + s, :] for s in range(4)]
            for r, value in enumerate(swap_blocks(v)):
                rows[r].append(value)
        modes = jnp.concatenate([jnp.concatenate(row, axis=1) for row in rows], axis=0)
        sf[n, u] = expand(modes).reshape(GX, 64, 256)

        def step(v, carry):
            other = (i + v) % GX
            send(sf.at[n, u, other], rf.at[n, u, i], f_send.at[n, u], f_recv.at[n, u], other, j)
            return carry

        lax.fori_loop(0, GX, step, 0)

    def unpack_cells(n, u):
        wait(rf.at[n, u], f_recv.at[n, u])
        for t in range(2):
            for h in range(2):
                v = [rf[n, u, 4 * h + b, :, pl.ds(128 * t, 128)] for b in range(4)]
                for s, value in enumerate(swap_blocks(v)):
                    result[n, :, 8 * u + 4 * t + s, pl.ds(128 * h, 128)] = value

    loads[0].wait()
    pack_cells(0, 0)
    pl.semaphore_wait(barrier, GX + 3 * GY)
    send_cells(0, 0)
    pack_cells(0, 1)
    send_cells(0, 1)
    loads[1].wait()
    for u in range(2):
        pack_cells(1, u)
        send_cells(1, u)

    column = lax.broadcasted_iota(jnp.int32, (128, 4096), 1)
    row = lax.broadcasted_iota(jnp.int32, (128, 4096), 0)
    spread[...] = jnp.where(column // 32 == row, 1.0, 0.0).astype(BF16)

    loads[2].wait()
    for n in range(2):
        for u in range(2):
            project_x(n, u)
        send_columns(n, sb, rb, b_send, b_recv)
    loads[3].wait()
    for n in range(2):
        project_y(n)
    mix()
    tiled = mix_back()
    loads[4].wait()
    for n in range(2):
        expand_y(n)
    for n in range(2):
        wait(re.at[n], e_recv.at[n])
        for u in range(2):
            expand_x(n, u)
    outer(tiled)
    stores = [pltpu.make_async_copy(wgrad, weight_grad, out_sem.at[2])]
    stores[0].start()
    for n, target in enumerate([output_field, field_grad]):
        for u in range(2):
            unpack_cells(n, u)
        store = pltpu.make_async_copy(result.at[n], target, out_sem.at[n])
        store.start()
        stores.append(store)

    for n in range(2):
        for u in range(2):
            wait(sa.at[n, u, pl.ds(0, GX - 1)], a_send.at[n, u])
            wait(sf.at[n, u, pl.ds(0, GX - 1)], f_send.at[n, u])
        wait(sb.at[n, pl.ds(0, GY - 1)], b_send.at[n])
        wait(se.at[n, pl.ds(0, GY - 1)], e_send.at[n])

    inside = i == j // 4

    @pl.when(inside)
    def _():
        for n in range(2):
            wait(sc.at[n, pl.ds(0, GY - 1)], c_send.at[n])
            wait(rd.at[n, pl.ds(0, GY - 1)], d_send.at[n])

    @pl.when(jnp.logical_not(inside))
    def _():
        for n in range(2):
            wait(sc.at[n], c_send.at[n])
            wait(rd.at[n], d_send.at[n])

    for store in stores:
        store.wait()


def body(field, weights, cotangent):
    high, low = split_table(basis_table())
    table_in = jnp.asarray(np.concatenate([high, low], axis=0))
    table_out = jnp.asarray(np.concatenate([high.T, low.T, high.T], axis=1))
    shape = jax.ShapeDtypeStruct
    anywhere = pl.BlockSpec(memory_space=pl.ANY)
    vmem = pltpu.VMEM
    dma = pltpu.SemaphoreType.DMA
    cell_block = vmem((2, 2, GX, 64, 256), F32)
    column_block = vmem((2, GY, 16, 128), F32)
    out = pl.pallas_call(
        kernel,
        out_shape=(
            shape(field.shape, F32),
            shape(field.shape, F32),
            shape((4, 4, 4, 8, 1024), F32),
        ),
        in_specs=[anywhere] * 5,
        out_specs=(anywhere,) * 3,
        scratch_shapes=[
            vmem((2, 64, 16, 256), F32),
            vmem((4, 4, 4, 8, 1024), F32),
            vmem((256, N), BF16),
            vmem((N, 384), BF16),
            vmem((128, 4096), BF16),
            vmem((128, 4096), F32),
            vmem((4, 4, 4, 8, 1024), F32),
            vmem((2, 64, 16, 256), F32),
            cell_block, cell_block,
            column_block, column_block,
            vmem((2, GY, 4, 128), F32), vmem((2, GX, 4, 4, 128), F32),
            vmem((2, GX, 4, 4, 128), F32), vmem((2, GY, 4, 128), F32),
            column_block, column_block,
            cell_block, cell_block,
            dma((5,)), dma((3,)),
            dma((2, 2)), dma((2, 2)),
            dma((2,)), dma((2,)),
            dma((2,)), dma((2,)),
            dma((2,)), dma((2,)),
            dma((2,)), dma((2,)),
            dma((2, 2)), dma((2, 2)),
        ],
        compiler_params=pltpu.CompilerParams(
            collective_id=0, has_side_effects=True, vmem_limit_bytes=56 * 1024 * 1024
        ),
        name="spectral",
    )(field, cotangent, weights.reshape(4, 4, 4, 8, 1024), table_in, table_out)
    return out[0], out[1], out[2].reshape(weights.shape)


def solution(mesh):
    in_specs = (P("gx", "gy", None), P("gy", "gx", None, None), P("gx", "gy", None))
    out_specs = (P("gx", "gy", None), P("gx", "gy", None), P("gy", "gx", None, None))
    return jax.shard_map(body, mesh=mesh, in_specs=in_specs, out_specs=out_specs, check_vma=False)
```

time: 313 us -> 111 us (0.35); the launches traced: 308 us -> 110 us
  Pallas kernels: 0 us -> 105 us
  local copies, waits for them, and re-layouts: 94.4 us -> 4.71 us
  blocking collectives: 87 us -> 0 us
  waiting for transfers between devices: 44.3 us -> 0 us
  matrix products: 34.4 us -> 0 us
  other arithmetic: 30.5 us -> 0 us
  starting transfers between devices: 16.1 us -> 0 us
    pallas_call x0 -> x1, Pallas kernels: none -> 105 us  [body(): pl.pallas_call(kernel, out_shape=(shape(field.shape, F32), shape(field.sh...]
    all_to_all x5 -> x0, blocking collectives: 87 us -> none  [the longest x1 27.1 us: project(): lax.all_to_all(xmodes, 'gy', split_axis=1, concat_axis=2, tiled=True)]
    all_to_all x3 -> x0, waiting for transfers between devices: 44.3 us -> none  [the longest x1 27.5 us: project(): cells = lax.all_to_all(pair, 'gx', split_axis=3, concat_axis=1, tiled=True)]
    unnamed x26 -> x7, local copies, waits for them, and re-layouts: 45.4 us -> 4.71 us
    dot_general x6 -> x0, matrix products: 34.4 us -> none  [the longest x1 15.4 us: body(): jnp.einsum('abzio,abzo->abzi', split_weights, grads, precision=lax.Precis...]
    all_to_all x8 -> x0, other arithmetic: 22 us -> none  [the longest x1 7.22 us: expand(): return lax.all_to_all(cells, 'gx', split_axis=1, concat_axis=3, tiled=True)]
    all_to_all x15 -> x0, local copies, waits for them, and re-layouts: 20.6 us -> none  [the longest x3 10.7 us: project(): cells = lax.all_to_all(pair, 'gx', split_axis=3, concat_axis=1, tiled=True)]
    all_to_all x3 -> x0, starting transfers between devices: 16.1 us -> none  [the longest x1 7.97 us: project(): cells = lax.all_to_all(pair, 'gx', split_axis=3, concat_axis=1, tiled=True)]
  transfers between devices with their start and end apart: 3 -> 0, of which waited for: 3 -> 0; matrix products, arithmetic and copies ran while one was open for 6% -> 0% of each run, Pallas kernels for 0% -> 0%
where the time goes in v2:
time: 111 us; the launch traced here: 110 us
  Pallas kernels  105 us (95%)
  local copies, waits for them, and re-layouts  4.71 us (4%)
    pallas_call x1, Pallas kernels, body(): pl.pallas_call(kernel, out_shape=(shape(field.shape, F32), shape(field.sh...  105 us
    unnamed x7, local copies, waits for them, and re-layouts  4.71 us

profile of v2, /device:TPU:1, one launch (start us, length us, event | category | flops | bytes accessed | tf_op | source)
XLA Modules:
  0.0 110.2 jit_solution(7040806584530579785)
XLA Ops:
  0.6 104.9 %spectral.1 = (f32[64,16,256]{2,1,0:T(8,128)}, f32[64,16,256]{2,1,0:T(8,128)}, f32[4,4,4,8,1024]{4,3,2,1,0:T(8,128)}) custom-call(f32[64,16,256]{2,1,0:T(8,128)} %field.1, f32[64,16,256]{2,1,0:T(8,128)} %cotangent.1, f32[4,4,4,8,1024]{4,3,2,1,0:T(8,128)} %bitcast.2, bf16[256,512]{1,0:T(8,128)(2,1)} %constant.4.clone.table_in, ...), custom_call_target="tpu_custom_call" | custom-call | tf_op jit(solution)/shard_map/spectral/pallas_call | solution.py:333
  105.5 0.0 copy-start.1
  105.5 0.0 copy-start
  105.5 2.4 %copy.11 = f32[64,16,256]{2,1,0:T(8,128)} copy(f32[64,16,256]{2,1,0:T(8,128)} %get-tuple-element.12) | data formatting | bytes 2097152
  107.9 0.0 copy-done.1
  107.9 1.0 copy.12
  108.9 0.0 copy-done
  108.9 1.3 %copy.13 = f32[4,16,8,1024]{3,2,1,0:T(8,128)} copy(f32[4,16,8,1024]{3,2,1,0:T(8,128)S(1)} %bitcast.3) | data formatting | bytes 4194304
Async XLA Ops:
  105.5 2.4 %copy-start.1 = (f32[64,16,256]{2,1,0:T(8,128)S(1)}, f32[64,16,256]{2,1,0:T(8,128)}, u32[]{:S(2)}) copy-start(f32[64,16,256]{2,1,0:T(8,128)} %get-tuple-element.13) | copy-start | bytes 3145732
  105.5 3.4 %copy-start = (f32[4,4,4,8,1024]{4,3,2,1,0:T(8,128)S(1)}, f32[4,4,4,8,1024]{4,3,2,1,0:T(8,128)}, u32[]{:S(2)}) copy-start(f32[4,4,4,8,1024]{4,3,2,1,0:T(8,128)} %get-tuple-element.8) | copy-start | bytes 6291460

commit v3 on v2

--- a/solution.py
+++ b/solution.py
@@ -12,6 +12,7 @@
 MODES = 64
 GX = 8
 GY = 32
+ORDER = (1, 2, 3, 4, 5, 6, 7)
 F32 = jnp.float32
 BF16 = jnp.bfloat16
 MESH = pl.DeviceIdType.MESH
@@ -36,6 +37,12 @@
 def halves(value):
     high = value.astype(BF16)
     return high, (value - high.astype(F32)).astype(BF16)
+
+
+def spread_matrix():
+    column = lax.broadcasted_iota(jnp.int32, (128, 4096), 1)
+    row = lax.broadcasted_iota(jnp.int32, (128, 4096), 0)
+    return jnp.where(column // 32 == row, 1.0, 0.0).astype(BF16)
 
 
 def dot(a, b):
@@ -59,10 +66,10 @@
 
 
 def kernel(
-    field, cotangent, weights, table_in, table_out,
-    output_field, field_grad, weight_grad,
-    cells, w, fwd, inv, spread, expanded, wgrad, result,
-    sa, ra, sb, rb, sc, rc, sd, rd, se, re, sf, rf,
+    field, cotangent, weights, table_in, table_out, table_in_y, table_out_y,
+    rf, weight_grad,
+    cells, w, fwd, inv, fwd_y, inv_y, spread, expanded, wgrad,
+    sa, ra, sb, rb, sc, rc, sd, rd, se, re, sf,
     in_sem, out_sem, a_send, a_recv, b_send, b_recv, c_send, c_recv,
     d_send, d_recv, e_send, e_recv, f_send, f_recv,
 ):
@@ -75,7 +82,7 @@
     loads = [
         pltpu.make_async_copy(src, dst, in_sem.at[n])
         for n, (src, dst) in enumerate(
-            [(field, cells.at[0]), (cotangent, cells.at[1]), (table_in, fwd), (weights, w), (table_out, inv)]
+            [(field, cells.at[0]), (cotangent, cells.at[1]), (table_in, fwd), (table_in_y, fwd_y), (weights, w), (table_out_y, inv_y), (table_out, inv)]
         )
     ]
     for load in loads:
@@ -124,42 +131,55 @@
                 for b, value in enumerate(swap_blocks(v)):
                     sa[n, u, 4 * h + b, :, pl.ds(128 * t, 128)] = value
 
-    def send_cells(n, u):
-        def step(v, carry):
+    def send_x(src, dst, send_sem, recv_sem, n, u, part):
+        rows = pl.ds(32 * part, 32)
+        for v in ORDER:
             other = (i + v) % GX
-            send(sa.at[n, u, other], ra.at[n, u, i], a_send.at[n, u], a_recv.at[n, u], other, j)
-            return carry
-
-        lax.fori_loop(0, GX, step, 0)
-
-    def project(data):
+            pltpu.make_async_remote_copy(
+                src_ref=src.at[n, u, other, rows], dst_ref=dst.at[n, u, i, rows],
+                send_sem=send_sem.at[n, u], recv_sem=recv_sem.at[n, u],
+                device_id=at(other, j), device_id_type=MESH,
+            ).start()
+        pltpu.make_async_copy(src.at[n, u, i, rows], dst.at[n, u, i, rows], recv_sem.at[n, u]).start()
+
+    def send_cells(n, u, part):
+        send_x(sa, ra, a_send, a_recv, n, u, part)
+
+    def send_result(n, u, part):
+        send_x(sf, rf, f_send, f_recv, n, u, part)
+
+    def project(table, data):
         high, low = halves(data)
-        first = dot(fwd[...], high)
-        return first[:128] + first[128:] + dot(fwd[:128], low)
-
-    def expand(data):
+        first = dot(table, high)
+        return first[:128] + first[128:] + dot(table[:128], low)
+
+    def expand(table, data):
         high, low = halves(data)
-        return dot(inv[...], jnp.concatenate([high, high, low], axis=0))
+        return dot(table, jnp.concatenate([high, high, low], axis=0))
 
     def project_x(n, u):
         wait(ra.at[n, u], a_recv.at[n, u])
-        modes = project(ra[n, u].reshape(N, 256))
+        modes = project(fwd[...], ra[n, u].reshape(N, 256))
         for t in range(2):
             v = [modes[32 * r : 32 * r + 32, 128 * t : 128 * t + 128] for r in range(4)]
             for s, value in enumerate(swap_blocks(v)):
-                sb[n, :, 8 * u + 4 * t + s, :] = value
-
-    def send_columns(n, src, dst, send_sem, recv_sem):
+                sb[n, u, :, 4 * t + s, :] = value
+        send_columns(n, u, sb, rb, b_send, b_recv)
+
+    def send_columns(n, u, src, dst, send_sem, recv_sem):
         def step(v, carry):
             other = (j + v) % GY
-            send(src.at[n, other], dst.at[n, j], send_sem.at[n], recv_sem.at[n], i, other)
+            send(src.at[n, u, other], dst.at[n, u, j], send_sem.at[n, u], recv_sem.at[n, u], i, other)
             return carry
 
         lax.fori_loop(0, GY, step, 0)
 
     def project_y(n):
-        wait(rb.at[n], b_recv.at[n])
-        modes = project(rb[n].reshape(N, 128))
+        parts = []
+        for u in range(2):
+            wait(rb.at[n, u], b_recv.at[n, u])
+            parts.append(project(fwd_y[:, pl.ds(256 * u, 256)], rb[n, u].reshape(256, 128)))
+        modes = parts[0] + parts[1]
         for a in range(4):
             sc[n, :, a, :] = modes[32 * a : 32 * a + 32]
 
@@ -223,84 +243,74 @@
             value = expanded[:, pl.ds(1024 * r, 1024)] * jnp.concatenate([tiled[r]] * 8, axis=1)
             wgrad[:, :, r] = value.reshape(4, 4, 8, 1024)
 
+
     def expand_y(n):
         wait(rd.at[n], d_recv.at[n])
         modes = jnp.concatenate([rd[n, :, a, :] for a in range(4)], axis=0)
-        se[n] = expand(modes).reshape(GY, 16, 128)
-        send_columns(n, se, re, e_send, e_recv)
+        for u in range(2):
+            rows = expand(inv_y[pl.ds(256 * u, 256), :], modes)
+            se[n, u] = rows.reshape(GY, 8, 128)
+            send_columns(n, u, se, re, e_send, e_recv)
 
     def expand_x(n, u):
+        wait(re.at[n, u], e_recv.at[n, u])
         rows = [[] for _ in range(4)]
         for t in range(2):
-            v = [re[n, :, 8 * u + 4 * t + s, :] for s in range(4)]
+            v = [re[n, u, :, 4 * t + s, :] for s in range(4)]
             for r, value in enumerate(swap_blocks(v)):
                 rows[r].append(value)
         modes = jnp.concatenate([jnp.concatenate(row, axis=1) for row in rows], axis=0)
-        sf[n, u] = expand(modes).reshape(GX, 64, 256)
-
-        def step(v, carry):
-            other = (i + v) % GX
-            send(sf.at[n, u, other], rf.at[n, u, i], f_send.at[n, u], f_recv.at[n, u], other, j)
-            return carry
-
-        lax.fori_loop(0, GX, step, 0)
-
-    def unpack_cells(n, u):
-        wait(rf.at[n, u], f_recv.at[n, u])
-        for t in range(2):
-            for h in range(2):
-                v = [rf[n, u, 4 * h + b, :, pl.ds(128 * t, 128)] for b in range(4)]
-                for s, value in enumerate(swap_blocks(v)):
-                    result[n, :, 8 * u + 4 * t + s, pl.ds(128 * h, 128)] = value
+        sf[n, u] = expand(inv[...], modes).reshape(GX, 64, 256)
 
     loads[0].wait()
     pack_cells(0, 0)
+    pack_cells(0, 1)
     pl.semaphore_wait(barrier, GX + 3 * GY)
-    send_cells(0, 0)
-    pack_cells(0, 1)
-    send_cells(0, 1)
+    for u in range(2):
+        for part in range(2):
+            send_cells(0, u, part)
     loads[1].wait()
     for u in range(2):
         pack_cells(1, u)
-        send_cells(1, u)
-
-    column = lax.broadcasted_iota(jnp.int32, (128, 4096), 1)
-    row = lax.broadcasted_iota(jnp.int32, (128, 4096), 0)
-    spread[...] = jnp.where(column // 32 == row, 1.0, 0.0).astype(BF16)
-
-    loads[2].wait()
+    spread[...] = spread_matrix()
+    for load in loads[2:]:
+        load.wait()
+
+    project_x(0, 0)
+    send_cells(1, 0, 0)
+    project_x(0, 1)
+    send_cells(1, 0, 1)
+    send_cells(1, 1, 0)
+    send_cells(1, 1, 1)
+    project_y(0)
+    project_x(1, 0)
+    project_x(1, 1)
+    mix()
+    project_y(1)
+    expand_y(0)
+    tiled = mix_back()
+    expand_x(0, 0)
+    send_result(0, 0, 0)
+    send_result(0, 0, 1)
+    expand_x(0, 1)
+    expand_y(1)
+    send_result(0, 1, 0)
+    send_result(0, 1, 1)
+    outer(tiled)
+    store = pltpu.make_async_copy(wgrad, weight_grad, out_sem.at[0])
+    store.start()
+    for u in range(2):
+        expand_x(1, u)
+        for part in range(2):
+            send_result(1, u, part)
+
     for n in range(2):
         for u in range(2):
-            project_x(n, u)
-        send_columns(n, sb, rb, b_send, b_recv)
-    loads[3].wait()
-    for n in range(2):
-        project_y(n)
-    mix()
-    tiled = mix_back()
-    loads[4].wait()
-    for n in range(2):
-        expand_y(n)
-    for n in range(2):
-        wait(re.at[n], e_recv.at[n])
-        for u in range(2):
-            expand_x(n, u)
-    outer(tiled)
-    stores = [pltpu.make_async_copy(wgrad, weight_grad, out_sem.at[2])]
-    stores[0].start()
-    for n, target in enumerate([output_field, field_grad]):
-        for u in range(2):
-            unpack_cells(n, u)
-        store = pltpu.make_async_copy(result.at[n], target, out_sem.at[n])
-        store.start()
-        stores.append(store)
-
-    for n in range(2):
-        for u in range(2):
+            wait(rf.at[n, u], f_recv.at[n, u])
             wait(sa.at[n, u, pl.ds(0, GX - 1)], a_send.at[n, u])
+            wait(sb.at[n, u, pl.ds(0, GY - 1)], b_send.at[n, u])
+            wait(se.at[n, u, pl.ds(0, GY - 1)], e_send.at[n, u])
             wait(sf.at[n, u, pl.ds(0, GX - 1)], f_send.at[n, u])
-        wait(sb.at[n, pl.ds(0, GY - 1)], b_send.at[n])
-        wait(se.at[n, pl.ds(0, GY - 1)], e_send.at[n])
 
     inside = i == j // 4
 
@@ -316,57 +326,105 @@
             wait(sc.at[n], c_send.at[n])
             wait(rd.at[n], d_send.at[n])
 
+    store.wait()
+
+
+def finish_kernel(
+    received, grad, output_field, field_grad, weight_grad,
+    cells, result, passed, load_sem, out_sem, grad_sem, pass_sem,
+):
+    loads = [
+        pltpu.make_async_copy(received.at[n, u], cells.at[n, u], load_sem.at[n, u])
+        for n in range(2)
+        for u in range(2)
+    ]
+    passes = [pltpu.make_async_copy(grad.at[a], passed.at[a], grad_sem.at[a]) for a in range(4)]
+    for load in loads[:2] + passes + loads[2:]:
+        load.start()
+    stores = []
+    for n, target in enumerate([output_field, field_grad]):
+        for u in range(2):
+            loads[2 * n + u].wait()
+            for t in range(2):
+                for h in range(2):
+                    v = [cells[n, u, 4 * h + b, :, pl.ds(128 * t, 128)] for b in range(4)]
+                    for s, value in enumerate(swap_blocks(v)):
+                        result[n, :, 8 * u + 4 * t + s, pl.ds(128 * h, 128)] = value
+        stores.append(pltpu.make_async_copy(result.at[n], target, out_sem.at[n]))
+        stores[-1].start()
+        for a in (2 * n, 2 * n + 1):
+            passes[a].wait()
+            stores.append(pltpu.make_async_copy(passed.at[a], weight_grad.at[a], pass_sem.at[a]))
+            stores[-1].start()
     for store in stores:
         store.wait()
 
 
 def body(field, weights, cotangent):
     high, low = split_table(basis_table())
-    table_in = jnp.asarray(np.concatenate([high, low], axis=0))
-    table_out = jnp.asarray(np.concatenate([high.T, low.T, high.T], axis=1))
+    table_in = np.concatenate([high, low], axis=0)
+    table_out = np.concatenate([high.T, low.T, high.T], axis=1)
+    table_in_y = table_in.reshape(256, GY, 2, 8).transpose(0, 2, 1, 3).reshape(256, N)
+    table_out_y = table_out.reshape(GY, 2, 8, 384).transpose(1, 0, 2, 3).reshape(N, 384)
+    tables = [jnp.asarray(t) for t in (table_in, table_out, table_in_y, table_out_y)]
     shape = jax.ShapeDtypeStruct
     anywhere = pl.BlockSpec(memory_space=pl.ANY)
     vmem = pltpu.VMEM
     dma = pltpu.SemaphoreType.DMA
     cell_block = vmem((2, 2, GX, 64, 256), F32)
-    column_block = vmem((2, GY, 16, 128), F32)
-    out = pl.pallas_call(
+    column_block = vmem((2, 2, GY, 8, 128), F32)
+    received, grad = pl.pallas_call(
         kernel,
-        out_shape=(
-            shape(field.shape, F32),
-            shape(field.shape, F32),
-            shape((4, 4, 4, 8, 1024), F32),
-        ),
-        in_specs=[anywhere] * 5,
-        out_specs=(anywhere,) * 3,
+        out_shape=(shape((2, 2, GX, 64, 256), F32), shape((4, 4, 4, 8, 1024), F32)),
+        in_specs=[anywhere] * 7,
+        out_specs=(anywhere,) * 2,
         scratch_shapes=[
             vmem((2, 64, 16, 256), F32),
             vmem((4, 4, 4, 8, 1024), F32),
             vmem((256, N), BF16),
             vmem((N, 384), BF16),
+            vmem((256, N), BF16),
+            vmem((N, 384), BF16),
             vmem((128, 4096), BF16),
             vmem((128, 4096), F32),
             vmem((4, 4, 4, 8, 1024), F32),
-            vmem((2, 64, 16, 256), F32),
             cell_block, cell_block,
             column_block, column_block,
             vmem((2, GY, 4, 128), F32), vmem((2, GX, 4, 4, 128), F32),
             vmem((2, GX, 4, 4, 128), F32), vmem((2, GY, 4, 128), F32),
             column_block, column_block,
-            cell_block, cell_block,
-            dma((5,)), dma((3,)),
+            cell_block,
+            dma((7,)), dma((1,)),
+            dma((2, 2)), dma((2, 2)),
             dma((2, 2)), dma((2, 2)),
             dma((2,)), dma((2,)),
             dma((2,)), dma((2,)),
-            dma((2,)), dma((2,)),
-            dma((2,)), dma((2,)),
+            dma((2, 2)), dma((2, 2)),
             dma((2, 2)), dma((2, 2)),
         ],
         compiler_params=pltpu.CompilerParams(
             collective_id=0, has_side_effects=True, vmem_limit_bytes=56 * 1024 * 1024
         ),
         name="spectral",
-    )(field, cotangent, weights.reshape(4, 4, 4, 8, 1024), table_in, table_out)
+    )(field, cotangent, weights.reshape(4, 4, 4, 8, 1024), *tables)
+    out = pl.pallas_call(
+        finish_kernel,
+        out_shape=(
+            shape(field.shape, F32),
+            shape(field.shape, F32),
+            shape((4, 4, 4, 8, 1024), F32),
+        ),
+        in_specs=[anywhere] * 2,
+        out_specs=(anywhere,) * 3,
+        scratch_shapes=[
+            cell_block,
+            vmem((2, 64, 16, 256), F32),
+            vmem((4, 4, 4, 8, 1024), F32),
+            dma((2, 2)), dma((2,)), dma((4,)), dma((4,)),
+        ],
+        compiler_params=pltpu.CompilerParams(vmem_limit_bytes=56 * 1024 * 1024),
+        name="finish",
+    )(received, grad)
     return out[0], out[1], out[2].reshape(weights.shape)
 
 

time: 111 us -> 103 us (0.928)
  local copies, waits for them, and re-layouts: 4.71 us -> 0 us
  Pallas kernels: 105 us -> 102 us
    unnamed x7 -> x0, local copies, waits for them, and re-layouts: 4.71 us -> none
    pallas_call x1 -> x2, Pallas kernels: 105 us -> 102 us  [the longest x1 96.3 us: body(): pl.pallas_call(kernel, out_shape=(shape((2, 2, GX, 64, 256), F32), shape(...]
where the time goes in v3:
time: 103 us
  Pallas kernels  102 us (99%)
    pallas_call x1, Pallas kernels, body(): pl.pallas_call(kernel, out_shape=(shape((2, 2, GX, 64, 256), F32), shape(...  96.3 us
    pallas_call x1, Pallas kernels, body(): pl.pallas_call(finish_kernel, out_shape=(shape(field.shape, F32), shape(f...  5.88 us

profile of v3, /device:TPU:1, one launch (start us, length us, event | category | flops | bytes accessed | tf_op | source)
XLA Modules:
  0.0 102.9 jit_solution(8658366616453254562)
XLA Ops:
  0.6 96.3 %spectral.1 = (f32[2,2,8,64,256]{4,3,2,1,0:T(8,128)}, f32[4,4,4,8,1024]{4,3,2,1,0:T(8,128)}) custom-call(f32[64,16,256]{2,1,0:T(8,128)} %field.1, f32[64,16,256]{2,1,0:T(8,128)} %cotangent.1, f32[4,4,4,8,1024]{4,3,2,1,0:T(8,128)} %bitcast.2, bf16[256,512]{1,0:T(8,128)(2,1)} %constant.8.clone.table_in, bf16[512,384]{1,0:T(8,128)(2,1)} %constant.9.clone.table_out, ...), custom_call_target="tpu_custom_call" | custom-call | tf_op jit(solution)/shard_map/spectral/pallas_call | solution.py:376
  97.0 5.9 %finish.1 = (f32[64,16,256]{2,1,0:T(8,128)}, f32[64,16,256]{2,1,0:T(8,128)}, f32[4,4,4,8,1024]{4,3,2,1,0:T(8,128)}) custom-call(f32[2,2,8,64,256]{4,3,2,1,0:T(8,128)} %get-tuple-element.8.received, f32[4,4,4,8,1024]{4,3,2,1,0:T(8,128)} %get-tuple-element.9.grad), custom_call_target="tpu_custom_call" | custom-call | tf_op jit(solution)/shard_map/finish/pallas_call | solution.py:410

commit v4 on v3

--- a/solution.py
+++ b/solution.py
@@ -12,7 +12,6 @@
 MODES = 64
 GX = 8
 GY = 32
-ORDER = (1, 2, 3, 4, 5, 6, 7)
 F32 = jnp.float32
 BF16 = jnp.bfloat16
 MESH = pl.DeviceIdType.MESH
@@ -125,28 +124,26 @@
         pltpu.make_async_copy(ref, ref, sem).wait()
 
     def pack_cells(n, u):
-        for t in range(2):
-            for h in range(2):
-                v = [cells[n, :, 8 * u + 4 * t + s, pl.ds(128 * h, 128)] for s in range(4)]
-                for b, value in enumerate(swap_blocks(v)):
-                    sa[n, u, 4 * h + b, :, pl.ds(128 * t, 128)] = value
-
-    def send_x(src, dst, send_sem, recv_sem, n, u, part):
-        rows = pl.ds(32 * part, 32)
-        for v in ORDER:
+        for h in range(2):
+            v = [cells[n, :, 4 * u + s, pl.ds(128 * h, 128)] for s in range(4)]
+            for b, value in enumerate(swap_blocks(v)):
+                sa[n, u, 4 * h + b] = value
+
+    def send_x(src, dst, send_sem, recv_sem, n, u):
+        for v in range(1, GX):
             other = (i + v) % GX
             pltpu.make_async_remote_copy(
-                src_ref=src.at[n, u, other, rows], dst_ref=dst.at[n, u, i, rows],
+                src_ref=src.at[n, u, other], dst_ref=dst.at[n, u, i],
                 send_sem=send_sem.at[n, u], recv_sem=recv_sem.at[n, u],
                 device_id=at(other, j), device_id_type=MESH,
             ).start()
-        pltpu.make_async_copy(src.at[n, u, i, rows], dst.at[n, u, i, rows], recv_sem.at[n, u]).start()
-
-    def send_cells(n, u, part):
-        send_x(sa, ra, a_send, a_recv, n, u, part)
-
-    def send_result(n, u, part):
-        send_x(sf, rf, f_send, f_recv, n, u, part)
+        pltpu.make_async_copy(src.at[n, u, i], dst.at[n, u, i], recv_sem.at[n, u]).start()
+
+    def send_cells(n, u):
+        send_x(sa, ra, a_send, a_recv, n, u)
+
+    def send_result(n, u):
+        send_x(sf, rf, f_send, f_recv, n, u)
 
     def project(table, data):
         high, low = halves(data)
@@ -159,11 +156,10 @@
 
     def project_x(n, u):
         wait(ra.at[n, u], a_recv.at[n, u])
-        modes = project(fwd[...], ra[n, u].reshape(N, 256))
-        for t in range(2):
-            v = [modes[32 * r : 32 * r + 32, 128 * t : 128 * t + 128] for r in range(4)]
-            for s, value in enumerate(swap_blocks(v)):
-                sb[n, u, :, 4 * t + s, :] = value
+        modes = project(fwd[...], ra[n, u].reshape(N, 128))
+        v = [modes[32 * r : 32 * r + 32] for r in range(4)]
+        for s, value in enumerate(swap_blocks(v)):
+            sb[n, u, :, s, :] = value
         send_columns(n, u, sb, rb, b_send, b_recv)
 
     def send_columns(n, u, src, dst, send_sem, recv_sem):
@@ -176,9 +172,13 @@
 
     def project_y(n):
         parts = []
-        for u in range(2):
-            wait(rb.at[n, u], b_recv.at[n, u])
-            parts.append(project(fwd_y[:, pl.ds(256 * u, 256)], rb[n, u].reshape(256, 128)))
+        for half in range(2):
+            rows = []
+            for u in (2 * half, 2 * half + 1):
+                wait(rb.at[n, u], b_recv.at[n, u])
+                rows += [rb[n, u, :, s, :] for s in range(4)]
+            table = fwd_y[:, pl.ds(256 * half, 256)]
+            parts.append(project(table, jnp.concatenate(rows, axis=0)))
         modes = parts[0] + parts[1]
         for a in range(4):
             sc[n, :, a, :] = modes[32 * a : 32 * a + 32]
@@ -247,65 +247,63 @@
     def expand_y(n):
         wait(rd.at[n], d_recv.at[n])
         modes = jnp.concatenate([rd[n, :, a, :] for a in range(4)], axis=0)
-        for u in range(2):
-            rows = expand(inv_y[pl.ds(256 * u, 256), :], modes)
-            se[n, u] = rows.reshape(GY, 8, 128)
+        for u in range(4):
+            rows = expand(inv_y[pl.ds(128 * u, 128), :], modes)
+            for s in range(4):
+                se[n, u, :, s, :] = rows[32 * s : 32 * s + 32]
             send_columns(n, u, se, re, e_send, e_recv)
 
     def expand_x(n, u):
         wait(re.at[n, u], e_recv.at[n, u])
-        rows = [[] for _ in range(4)]
-        for t in range(2):
-            v = [re[n, u, :, 4 * t + s, :] for s in range(4)]
-            for r, value in enumerate(swap_blocks(v)):
-                rows[r].append(value)
-        modes = jnp.concatenate([jnp.concatenate(row, axis=1) for row in rows], axis=0)
-        sf[n, u] = expand(inv[...], modes).reshape(GX, 64, 256)
+        v = [re[n, u, :, s, :] for s in range(4)]
+        modes = jnp.concatenate(swap_blocks(v), axis=0)
+        sf[n, u] = expand(inv[...], modes).reshape(GX, 64, 128)
 
     loads[0].wait()
-    pack_cells(0, 0)
-    pack_cells(0, 1)
+    for u in range(4):
+        pack_cells(0, u)
     pl.semaphore_wait(barrier, GX + 3 * GY)
-    for u in range(2):
-        for part in range(2):
-            send_cells(0, u, part)
+    for u in range(4):
+        send_cells(0, u)
     loads[1].wait()
-    for u in range(2):
+    for u in range(4):
         pack_cells(1, u)
     spread[...] = spread_matrix()
     for load in loads[2:]:
         load.wait()
 
     project_x(0, 0)
-    send_cells(1, 0, 0)
     project_x(0, 1)
-    send_cells(1, 0, 1)
-    send_cells(1, 1, 0)
-    send_cells(1, 1, 1)
+    send_cells(1, 0)
+    send_cells(1, 1)
+    project_x(0, 2)
+    project_x(0, 3)
+    send_cells(1, 2)
+    send_cells(1, 3)
     project_y(0)
-    project_x(1, 0)
-    project_x(1, 1)
+    for u in range(4):
+        project_x(1, u)
     mix()
     project_y(1)
     expand_y(0)
     tiled = mix_back()
-    expand_x(0, 0)
-    send_result(0, 0, 0)
-    send_result(0, 0, 1)
-    expand_x(0, 1)
+    for u in range(2):
+        expand_x(0, u)
+        send_result(0, u)
+    for u in range(2, 4):
+        expand_x(0, u)
     expand_y(1)
-    send_result(0, 1, 0)
-    send_result(0, 1, 1)
+    for u in range(2, 4):
+        send_result(0, u)
     outer(tiled)
     store = pltpu.make_async_copy(wgrad, weight_grad, out_sem.at[0])
     store.start()
-    for u in range(2):
+    for u in range(4):
         expand_x(1, u)
-        for part in range(2):
-            send_result(1, u, part)
+        send_result(1, u)
 
     for n in range(2):
-        for u in range(2):
+        for u in range(4):
             wait(rf.at[n, u], f_recv.at[n, u])
             wait(sa.at[n, u, pl.ds(0, GX - 1)], a_send.at[n, u])
             wait(sb.at[n, u, pl.ds(0, GY - 1)], b_send.at[n, u])
@@ -336,26 +334,29 @@
     loads = [
         pltpu.make_async_copy(received.at[n, u], cells.at[n, u], load_sem.at[n, u])
         for n in range(2)
-        for u in range(2)
+        for u in range(4)
     ]
     passes = [pltpu.make_async_copy(grad.at[a], passed.at[a], grad_sem.at[a]) for a in range(4)]
-    for load in loads[:2] + passes + loads[2:]:
+    for load in loads[:4] + passes + loads[4:]:
         load.start()
     stores = []
     for n, target in enumerate([output_field, field_grad]):
-        for u in range(2):
-            loads[2 * n + u].wait()
-            for t in range(2):
-                for h in range(2):
-                    v = [cells[n, u, 4 * h + b, :, pl.ds(128 * t, 128)] for b in range(4)]
-                    for s, value in enumerate(swap_blocks(v)):
-                        result[n, :, 8 * u + 4 * t + s, pl.ds(128 * h, 128)] = value
-        stores.append(pltpu.make_async_copy(result.at[n], target, out_sem.at[n]))
-        stores[-1].start()
-        for a in (2 * n, 2 * n + 1):
-            passes[a].wait()
-            stores.append(pltpu.make_async_copy(passed.at[a], weight_grad.at[a], pass_sem.at[a]))
-            stores[-1].start()
+        for u in range(4):
+            loads[4 * n + u].wait()
+            for h in range(2):
+                v = [cells[n, u, 4 * h + b] for b in range(4)]
+                for s, value in enumerate(swap_blocks(v)):
+                    result[n, :, 4 * u + s, pl.ds(128 * h, 128)] = value
+            if u % 2 == 1:
+                rows = pl.ds(4 * u - 4, 8)
+                stores.append(
+                    pltpu.make_async_copy(result.at[n, :, rows], target.at[:, rows], out_sem.at[n, u // 2])
+                )
+                stores[-1].start()
+                a = 2 * n + u // 2
+                passes[a].wait()
+                stores.append(pltpu.make_async_copy(passed.at[a], weight_grad.at[a], pass_sem.at[a]))
+                stores[-1].start()
     for store in stores:
         store.wait()
 
@@ -364,18 +365,18 @@
     high, low = split_table(basis_table())
     table_in = np.concatenate([high, low], axis=0)
     table_out = np.concatenate([high.T, low.T, high.T], axis=1)
-    table_in_y = table_in.reshape(256, GY, 2, 8).transpose(0, 2, 1, 3).reshape(256, N)
-    table_out_y = table_out.reshape(GY, 2, 8, 384).transpose(1, 0, 2, 3).reshape(N, 384)
+    table_in_y = table_in.reshape(256, GY, 4, 4).transpose(0, 2, 3, 1).reshape(256, N)
+    table_out_y = table_out.reshape(GY, 4, 4, 384).transpose(1, 2, 0, 3).reshape(N, 384)
     tables = [jnp.asarray(t) for t in (table_in, table_out, table_in_y, table_out_y)]
     shape = jax.ShapeDtypeStruct
     anywhere = pl.BlockSpec(memory_space=pl.ANY)
     vmem = pltpu.VMEM
     dma = pltpu.SemaphoreType.DMA
-    cell_block = vmem((2, 2, GX, 64, 256), F32)
-    column_block = vmem((2, 2, GY, 8, 128), F32)
+    cell_block = vmem((2, 4, GX, 64, 128), F32)
+    column_block = vmem((2, 4, GY, 4, 128), F32)
     received, grad = pl.pallas_call(
         kernel,
-        out_shape=(shape((2, 2, GX, 64, 256), F32), shape((4, 4, 4, 8, 1024), F32)),
+        out_shape=(shape((2, 4, GX, 64, 128), F32), shape((4, 4, 4, 8, 1024), F32)),
         in_specs=[anywhere] * 7,
         out_specs=(anywhere,) * 2,
         scratch_shapes=[
@@ -395,12 +396,12 @@
             column_block, column_block,
             cell_block,
             dma((7,)), dma((1,)),
-            dma((2, 2)), dma((2, 2)),
-            dma((2, 2)), dma((2, 2)),
+            dma((2, 4)), dma((2, 4)),
+            dma((2, 4)), dma((2, 4)),
             dma((2,)), dma((2,)),
             dma((2,)), dma((2,)),
-            dma((2, 2)), dma((2, 2)),
-            dma((2, 2)), dma((2, 2)),
+            dma((2, 4)), dma((2, 4)),
+            dma((2, 4)), dma((2, 4)),
         ],
         compiler_params=pltpu.CompilerParams(
             collective_id=0, has_side_effects=True, vmem_limit_bytes=56 * 1024 * 1024
@@ -420,7 +421,7 @@
             cell_block,
             vmem((2, 64, 16, 256), F32),
             vmem((4, 4, 4, 8, 1024), F32),
-            dma((2, 2)), dma((2,)), dma((4,)), dma((4,)),
+            dma((2, 4)), dma((2, 2)), dma((4,)), dma((4,)),
         ],
         compiler_params=pltpu.CompilerParams(vmem_limit_bytes=56 * 1024 * 1024),
         name="finish",

time: 103 us -> 102 us (level)
    pallas_call x1, Pallas kernels: 96.3 us -> 95.3 us  [body(): pl.pallas_call(kernel, out_shape=(shape((2, 4, GX, 64, 128), F32), shape(...]
where the time goes in v4:
time: 102 us; the launch traced here: 101 us
  Pallas kernels  101 us (99%)
    pallas_call x1, Pallas kernels, body(): pl.pallas_call(kernel, out_shape=(shape((2, 4, GX, 64, 128), F32), shape(...  95.3 us
    pallas_call x1, Pallas kernels, body(): pl.pallas_call(finish_kernel, out_shape=(shape(field.shape, F32), shape(f...  5.34 us

profile of v4, /device:TPU:1, one launch (start us, length us, event | category | flops | bytes accessed | tf_op | source)
XLA Modules:
  0.0 101.4 jit_solution(5341751305759688631)
XLA Ops:
  0.6 95.3 %spectral.1 = (f32[2,4,8,64,128]{4,3,2,1,0:T(8,128)}, f32[4,4,4,8,1024]{4,3,2,1,0:T(8,128)}) custom-call(f32[64,16,256]{2,1,0:T(8,128)} %field.1, f32[64,16,256]{2,1,0:T(8,128)} %cotangent.1, f32[4,4,4,8,1024]{4,3,2,1,0:T(8,128)} %bitcast.2, bf16[256,512]{1,0:T(8,128)(2,1)} %constant.8.clone.table_in, bf16[512,384]{1,0:T(8,128)(2,1)} %constant.9.clone.table_out, ...), custom_call_target="tpu_custom_call" | custom-call | tf_op jit(solution)/shard_map/spectral/pallas_call | solution.py:377
  95.9 5.3 %finish.1 = (f32[64,16,256]{2,1,0:T(8,128)}, f32[64,16,256]{2,1,0:T(8,128)}, f32[4,4,4,8,1024]{4,3,2,1,0:T(8,128)}) custom-call(f32[2,4,8,64,128]{4,3,2,1,0:T(8,128)} %get-tuple-element.8.received, f32[4,4,4,8,1024]{4,3,2,1,0:T(8,128)} %get-tuple-element.9.grad), custom_call_target="tpu_custom_call" | custom-call | tf_op jit(solution)/shard_map/finish/pallas_call | solution.py:411

commit v5 on v4

--- a/solution.py
+++ b/solution.py
@@ -12,6 +12,7 @@
 MODES = 64
 GX = 8
 GY = 32
+PEERS = ((1, 0), (0, 1), (3, 0), (2, 1), (1, 1), (2, 0), (3, 1))
 F32 = jnp.float32
 BF16 = jnp.bfloat16
 MESH = pl.DeviceIdType.MESH
@@ -130,8 +131,9 @@
                 sa[n, u, 4 * h + b] = value
 
     def send_x(src, dst, send_sem, recv_sem, n, u):
-        for v in range(1, GX):
-            other = (i + v) % GX
+        for dy, dx in PEERS:
+            dy = jnp.where(j % 2 == 0, dy, 4 - dy)
+            other = (i // 2 + dy) % 4 * 2 + (i + dx) % 2
             pltpu.make_async_remote_copy(
                 src_ref=src.at[n, u, other], dst_ref=dst.at[n, u, i],
                 send_sem=send_sem.at[n, u], recv_sem=recv_sem.at[n, u],

time: 102 us -> 103 us (level)
    pallas_call x1, Pallas kernels: 95.3 us -> 97 us  [body(): pl.pallas_call(kernel, out_shape=(shape((2, 4, GX, 64, 128), F32), shape(...]
where the time goes in v5:
time: 103 us
  Pallas kernels  102 us (99%)
    pallas_call x1, Pallas kernels, body(): pl.pallas_call(kernel, out_shape=(shape((2, 4, GX, 64, 128), F32), shape(...  97 us
    pallas_call x1, Pallas kernels, body(): pl.pallas_call(finish_kernel, out_shape=(shape(field.shape, F32), shape(f...  5.34 us

profile of v5, /device:TPU:1, one launch (start us, length us, event | category | flops | bytes accessed | tf_op | source)
XLA Modules:
  0.0 103.2 jit_solution(18081182061832530966)
XLA Ops:
  0.6 97.0 %spectral.1 = (f32[2,4,8,64,128]{4,3,2,1,0:T(8,128)}, f32[4,4,4,8,1024]{4,3,2,1,0:T(8,128)}) custom-call(f32[64,16,256]{2,1,0:T(8,128)} %field.1, f32[64,16,256]{2,1,0:T(8,128)} %cotangent.1, f32[4,4,4,8,1024]{4,3,2,1,0:T(8,128)} %bitcast.2, bf16[256,512]{1,0:T(8,128)(2,1)} %constant.8.clone.table_in, bf16[512,384]{1,0:T(8,128)(2,1)} %constant.9.clone.table_out, ...), custom_call_target="tpu_custom_call" | custom-call | tf_op jit(solution)/shard_map/spectral/pallas_call | solution.py:379
  97.7 5.3 %finish.1 = (f32[64,16,256]{2,1,0:T(8,128)}, f32[64,16,256]{2,1,0:T(8,128)}, f32[4,4,4,8,1024]{4,3,2,1,0:T(8,128)}) custom-call(f32[2,4,8,64,128]{4,3,2,1,0:T(8,128)} %get-tuple-element.8.received, f32[4,4,4,8,1024]{4,3,2,1,0:T(8,128)} %get-tuple-element.9.grad), custom_call_target="tpu_custom_call" | custom-call | tf_op jit(solution)/shard_map/finish/pallas_call | solution.py:413
